TPU v7x, 32 devices: a whole 2x2x4 slice. The times are simulated.
32 devices in a mesh: depth: 2 (over x), row: 4 (over y, core), col: 4 (over z).
Axes of the slice: x: 2, y: 2, z: 4, core: 2. Of those that a mesh axis runs over, the one named last changes fastest.
Arguments:
- hidden: bfloat16 [512, 28672], P('col', ('depth', 'row')), may hold values from -6 to 6
- upstream: bfloat16 [512, 14336], P(('depth', 'row'), 'col'), may hold values from -6 to 6
- weight: bfloat16 [28672, 14336], P(('depth', 'row'), 'col'), may hold values from -0.03125 to 0.03125
Outputs:
- input_grad: bfloat16 [512, 28672], P('col', ('depth', 'row'))
- weight_grad: bfloat16 [28672, 14336], P(('depth', 'row'), 'col')
All inputs are finite; a program needn't handle non-finite values.
Results may differ from a plain program's by a relative error of at most 0.012.
Values may be sent and summed in bfloat16 or wider, within the bound.
A program may use at most 192 MiB of HBM per device.

v0:
```python
import math

import jax
import jax.numpy as jnp
from jax import lax
from jax.sharding import PartitionSpec as P


def contract_features(left, weight):
    return lax.dot_general(
        left, weight, (((1,), (1,)), ((), ())), preferred_element_type=jnp.float32
    )


def local(hidden, upstream, weight):
    upstream_all = lax.all_gather(upstream, ("depth", "row"), axis=0, tiled=True)
    total_tokens = hidden.shape[0] * lax.axis_size("col")
    token_scale = 1.0 / math.sqrt(total_tokens)
    summed_weight = lax.dot_general(
        lax.all_gather(hidden, "col", axis=0, tiled=True),
        upstream_all,
        (((0,), (0,)), ((), ())),
        preferred_element_type=jnp.float32,
    )
    partial_terms = contract_features(upstream_all, weight)
    unit_share = lax.psum_scatter(
        partial_terms.astype(jnp.bfloat16), "col", scatter_dimension=1, tiled=True
    )
    input_grad = lax.all_to_all(unit_share, "col", split_axis=0, concat_axis=1, tiled=True)
    weight_grad = (summed_weight * token_scale).astype(jnp.bfloat16)
    return (input_grad, weight_grad)


def solution(mesh):
    in_specs = (P("col", ("depth", "row")), P(("depth", "row"), "col"), P(("depth", "row"), "col"))
    out_specs = (P("col", ("depth", "row")), P(("depth", "row"), "col"))
    return jax.shard_map(local, mesh=mesh, in_specs=in_specs, out_specs=out_specs, check_vma=False)
```

profile of v0, /device:TPU:0, one launch (start us, length us, event | category | flops | bytes accessed | tf_op | source)
XLA Modules:
  0.0 259.8 jit_solution(9786422540523699782)
XLA Ops:
  7.2 0.0 all-gather.3.cloned.1.call-start
  7.2 0.7 all-gather.3.cloned.1.call-update
  7.9 0.0 reduce-scatter.4.cloned.1.call-start
  7.9 39.2 %all-gather.3.cloned.1.call-done = bf16[512,3584]{1,0:T(8,128)(2,1)} async-done(((bf16[64,3584]{1,0:T(8,128)(2,1)}), bf16[512,3584]{1,0:T(8,128)(2,1)}) %all-gather.3.cloned.1.call-update) | async-done | bytes 3670032 | tf_op jit(solution)/shard_map/all_gather | solution.py:16
  47.1 20.5 %convolution_convert_fusion = bf16[512,3584]{1,0:T(8,128)(2,1)} fusion(bf16[512,3584]{1,0:T(8,128)(2,1)} %all-gather.3.cloned.1.call-done, bf16[3584,3584]{1,0:T(8,128)(2,1)} %param.5), kind=kOutput, calls=%fused_computation.1 | convolution fusion | flops 13155172352 | bytes 33030144 | tf_op jit(solution)/shard_map/dot_general | solution.py:10
  67.6 6.0 %copy.7 = bf16[512,3584]{0,1:T(8,128)(2,1)} copy(bf16[512,3584]{1,0:T(8,128)(2,1)} %convolution_convert_fusion) | data formatting | bytes 7340032
  73.6 0.0 reduce-scatter.4.cloned.1.call-update
  73.6 0.0 all-gather.5.cloned.1.call-start
  73.6 0.7 all-gather.5.cloned.1.call-update
  74.3 67.8 %reduce-scatter.4.cloned.1.call-done = bf16[896,512]{1,0:T(8,128)(2,1)} async-done(((bf16[3584,512]{1,0:T(8,128)(2,1)}), bf16[896,512]{1,0:T(8,128)(2,1)}) %reduce-scatter.4.cloned.1.call-update) | async-done | bytes 917520
  142.2 2.2 copy.8
  144.4 4.0 %all-to-all-start = ((bf16[4,128,896]{2,1,0:T(8,128)(2,1)}), bf16[4,128,896]{2,1,0:T(8,128)(2,1)S(1)}, u32[]{:S(2)}, u32[]{:S(2)}) async-start(bf16[4,128,896]{2,1,0:T(8,128)(2,1)} %bitcast), calls=%async_computation | async-start | bytes 1835008 | tf_op jit(solution)/shard_map/all_to_all | solution.py:29
  148.4 82.6 %all-gather.5.cloned.1.call-done = bf16[512,3584]{1,0:T(8,128)(2,1)} async-done(((bf16[128,3584]{1,0:T(8,128)(2,1)}), bf16[512,3584]{1,0:T(8,128)(2,1)}) %all-gather.5.cloned.1.call-update) | async-done | bytes 3670032 | tf_op jit(solution)/shard_map/all_gather | solution.py:20
  231.1 21.3 %multiply_convert_fusion = bf16[3584,3584]{1,0:T(8,128)(2,1)} fusion(bf16[512,3584]{1,0:T(8,128)(2,1)} %all-gather.5.cloned.1.call-done, bf16[512,3584]{1,0:T(8,128)(2,1)} %all-gather.3.cloned.1.call-done), kind=kOutput, calls=%fused_computation | convolution fusion | flops 13179027456 | bytes 33030144 | tf_op jit(solution)/shard_map/dot_general | solution.py:19
  252.3 0.0 all-to-all-done
  252.3 1.0 copy.9
Async XLA Ops:
  7.2 40.0 %all-gather.3.cloned.1.call-start = ((), (), s32[]{:S(2)}) async-start(), calls=%async_computation.2 | async-start | bytes 4128768 | tf_op jit(solution)/shard_map/all_gather | solution.py:16
  7.9 134.3 %reduce-scatter.4.cloned.1.call-start = ((), (), s32[]{:S(2)}) async-start(), calls=%async_computation.4 | async-start | bytes 4587520
  73.6 157.5 %all-gather.5.cloned.1.call-start = ((), (), s32[]{:S(2)}) async-start(), calls=%async_computation.3 | async-start | bytes 4587520 | tf_op jit(solution)/shard_map/all_gather | solution.py:20
  144.4 107.9 %all-to-all-start = ((bf16[4,128,896]{2,1,0:T(8,128)(2,1)}), bf16[4,128,896]{2,1,0:T(8,128)(2,1)S(1)}, u32[]{:S(2)}, u32[]{:S(2)}) async-start(bf16[4,128,896]{2,1,0:T(8,128)(2,1)} %bitcast), calls=%async_computation | async-start | bytes 1835008 | tf_op jit(solution)/shard_map/all_to_all | solution.py:29
Sparse Core Ops, SparseCore 0:
  9.9 37.2 all-gather.2
  73.7 68.4 reduce-scatter.3
  143.7 87.2 all-gather.4
where the time goes:
time: 260 us
  waiting for transfers between devices  191 us (73%)
  matrix products  41.7 us (16%)
  between operations  13.7 us (5%)
  local copies, waits for them, and re-layouts  9.16 us (4%)
  starting transfers between devices  4.17 us (2%)
    all_gather x1, waiting for transfers between devices, local(): lax.all_gather(hidden, 'col', axis=0, tiled=True)  82.6 us
    unnamed x4, waiting for transfers between devices  69.2 us
    all_gather x1, waiting for transfers between devices, local(): lax.all_gather(upstream, ('depth', 'row'), axis=0, tiled=True)  39.2 us
    dot_general x1, matrix products, local(): lax.dot_general(lax.all_gather(hidden, 'col', axis=0, tiled=True), upstre...  21.3 us
    dot_general x1, matrix products, contract_features(): lax.dot_general(left, weight, (((1,), (1,)), ((), ())), preferred_element...  20.5 us
    unnamed x2, local copies, waits for them, and re-layouts  8.16 us
  transfers between devices with their start and end apart: 4, of which 3 were waited for; matrix products, arithmetic and copies ran while one was open for 9% of the time, Pallas kernels for 0%

commit v1 on v0

v1 whole, which is shorter than its diff:
```python
import functools
import math

import jax
import jax.numpy as jnp
from jax import lax
from jax.experimental import pallas as pl
from jax.experimental.pallas import tpu as pltpu
from jax.sharding import PartitionSpec as P

MESH = pl.DeviceIdType.MESH
HALVES = 2
LAG = 2
VMEM_BYTES = 60 * 1024 * 1024


def exchange_kernel(
    sizes, hid, up, w, hall, uall, own, to_right, to_left,
    up_all, w_all, part, got,
    up_local, hid_local, w_sem, out_sem,
    up_send, up_recv, fwd_send, fwd_recv,
    ag_send, ag_recv, rs_send, rs_recv,
):
    n, depth_n, row_n, chunks = sizes
    group = depth_n * row_n
    pairs = group // 2
    rows = hid.shape[0]
    up_rows = up.shape[0]
    unit = part.shape[2]
    half = rows // HALVES
    depth, row, z = lax.axis_index("depth"), lax.axis_index("row"), lax.axis_index("col")
    me = depth * row_n + row
    partner = me + 1 - 2 * lax.rem(me, 2)

    def plane(i):
        return (lax.div(i, row_n), lax.rem(i, row_n), z)

    def line(way):
        return (depth, row, jnp.clip(z + (1 - 2 * way), 0, n - 1))

    place = (z, n - 1 - z)

    def block_of(way, e):
        return e if way == 0 else n - 1 - e

    barrier = pltpu.get_barrier_semaphore()
    for k in range(1, pairs):
        pl.semaphore_signal(barrier, inc=1, device_id=plane(lax.rem(me + 2 * k, group)), device_id_type=MESH)
    pl.semaphore_signal(barrier, inc=1, device_id=plane(partner), device_id_type=MESH)
    for way in range(2):
        @pl.when(place[way] < n - 1)
        def _():
            pl.semaphore_signal(barrier, inc=1, device_id=line(way), device_id_type=MESH)
    near = jnp.where(z > 0, 1, 0) + jnp.where(z < n - 1, 1, 0)
    pl.semaphore_wait(barrier, pairs + near)

    def up_at(i):
        return up_all.at[pl.ds(pl.multiple_of(i * up_rows, up_rows), up_rows), :]

    def up_copy(k, source):
        return pltpu.make_async_remote_copy(
            src_ref=up, dst_ref=up_at(source), send_sem=up_send.at[k], recv_sem=up_recv.at[k],
            device_id=plane(lax.rem(me + 2 * k, group)), device_id_type=MESH)

    def fwd_copy(k, source, first=False):
        return pltpu.make_async_remote_copy(
            src_ref=up if first else up_at(source), dst_ref=up_at(source),
            send_sem=fwd_send.at[k], recv_sem=fwd_recv.at[k],
            device_id=plane(partner), device_id_type=MESH)

    def hid_rows(ref, b, c):
        return ref.at[pl.ds(pl.multiple_of(b * rows + c * half, half), half), :]

    def ag_copy(way, s, c):
        b = jnp.clip(z - (1 - 2 * way) * (s - 1), 0, n - 1)
        src = hid.at[pl.ds(c * half, half), :] if s == 1 else hid_rows(hall, b, c)
        return pltpu.make_async_remote_copy(
            src_ref=src, dst_ref=hid_rows(hall, b, c),
            send_sem=ag_send.at[way, s - 1, c], recv_sem=ag_recv.at[way, s - 1, c],
            device_id=line(way), device_id_type=MESH)

    def ag_arrive(way, s, c):
        b = jnp.clip(z - (1 - 2 * way) * s, 0, n - 1)
        pltpu.make_async_remote_copy(
            src_ref=hid_rows(hall, b, c), dst_ref=hid_rows(hall, b, c),
            send_sem=ag_send.at[way, s - 1, c], recv_sem=ag_recv.at[way, s - 1, c],
            device_id=line(way), device_id_type=MESH).wait_recv()

    def ag_pass(s, c):
        for way in range(2):
            p = place[way]

            @pl.when(p >= s)
            def _():
                ag_arrive(way, s, c)
                if s + 1 <= n - 1:
                    @pl.when(p < n - 1)
                    def _():
                        ag_copy(way, s + 1, c).start()

    for c in range(HALVES):
        for way in range(2):
            @pl.when(place[way] < n - 1)
            def _():
                ag_copy(way, 1, c).start()
    for k in range(1, pairs):
        up_copy(k, me).start()
    fwd_copy(0, me, True).start()
    own_up = pltpu.make_async_copy(up, up_at(me), up_local)
    own_up.start()
    own_hid = pltpu.make_async_copy(hid, hall.at[pl.ds(pl.multiple_of(z * rows, rows), rows), :], hid_local)
    own_hid.start()

    def w_copy(j):
        return pltpu.make_async_copy(
            w.at[pl.ds(pl.multiple_of(j * unit, unit), unit), :], w_all.at[j], w_sem.at[j])

    for j in range(chunks):
        w_copy(j).start()

    for k in range(1, pairs):
        source = lax.rem(me - 2 * k + group, group)
        up_copy(k, source).wait_recv()
        fwd_copy(k, source).start()
    for c in range(HALVES):
        if n > 1:
            ag_pass(1, c)
    own_up.wait()
    for k in range(pairs):
        fwd_copy(k, lax.rem(partner - 2 * k + group, group)).wait_recv()
    keep_up = pltpu.make_async_copy(up_all, uall, out_sem)
    keep_up.start()

    def part_at(j, b):
        return part.at[j, pl.ds(pl.multiple_of(b * rows, rows), rows), :]

    def rs_copy(way, j, b):
        return pltpu.make_async_remote_copy(
            src_ref=part_at(j, b), dst_ref=got.at[way, j, b],
            send_sem=rs_send.at[way, j, b], recv_sem=rs_recv.at[way, j, b],
            device_id=line(way), device_id_type=MESH)

    def rs_add(way, j, b):
        rs_copy(way, j, b).wait_recv()
        return (part_at(j, b)[...].astype(jnp.float32) + got[way, j, b].astype(jnp.float32)).astype(part.dtype)

    def rs_hop(way, j, e):
        b = block_of(way, e)

        @pl.when(place[way] > 0)
        def _():
            part_at(j, b)[...] = rs_add(way, j, b)
        rs_copy(way, j, b).start()

    later = [(s, c) for s in range(2, n) for c in range(HALVES)]
    slot_of = [min(1 + 3 * i, chunks - 1) for i in range(len(later))]

    @pl.loop(0, chunks)
    def _(j):
        w_copy(j).wait()
        part[j] = lax.dot_general(
            up_all[...], w_all[j], (((1,), (1,)), ((), ())), preferred_element_type=jnp.float32
        ).astype(part.dtype)
        for way in range(2):
            p = place[way]

            @pl.when(p == 0)
            def _():
                if n >= 3:
                    rs_hop(way, j, n - 1)

            @pl.when((p > 0) & (p <= n - 3) & (j >= LAG))
            def _():
                rs_hop(way, j - LAG, n - 1)
        for (s, c), slot in zip(later, slot_of):
            if slot < chunks - 1:
                @pl.when(j == slot)
                def _():
                    ag_pass(s, c)

    for (s, c), slot in zip(later, slot_of):
        if slot >= chunks - 1 and s < n - 1:
            ag_pass(s, c)

    @pl.loop(max(chunks - LAG, 0), chunks)
    def _(j):
        for way in range(2):
            @pl.when((place[way] > 0) & (place[way] <= n - 3))
            def _():
                rs_hop(way, j, n - 1)

    for e in range(n - 2, 1, -1):
        @pl.loop(0, chunks)
        def _(j):
            for way in range(2):
                @pl.when(place[way] <= e - 2)
                def _():
                    rs_hop(way, j, e)

    for j in range(chunks):
        columns = pl.ds(j * unit, unit)
        own[:, columns] = part_at(j, z)[...]
        for way, out in ((0, to_right), (1, to_left)):
            p = place[way]
            b = jnp.clip(z + (1 - 2 * way), 0, n - 1)

            @pl.when((p > 0) & (p < n - 1))
            def _():
                out[:, columns] = rs_add(way, j, b)

            @pl.when((p == 0) | (p == n - 1))
            def _():
                out[:, columns] = part_at(j, b)[...]

    for (s, c), slot in zip(later, slot_of):
        if slot >= chunks - 1 and s == n - 1:
            ag_pass(s, c)

    for k in range(1, pairs):
        up_copy(k, me).wait_send()
    for k in range(pairs):
        fwd_copy(k, lax.rem(me - 2 * k + group, group), k == 0).wait_send()
    for way in range(2):
        for s in range(1, n):
            @pl.when((place[way] >= s - 1) & (place[way] < n - 1))
            def _():
                for c in range(HALVES):
                    ag_copy(way, s, c).wait_send()
        for e in range(2, n):
            @pl.when(place[way] <= e - 2)
            def _():
                @pl.loop(0, chunks)
                def _(j):
                    rs_copy(way, j, block_of(way, e)).wait_send()
    own_hid.wait()
    keep_up.wait()


def exchange(hidden, upstream, weight, n, depth_n, row_n):
    rows, units = hidden.shape
    up_rows, features = upstream.shape
    tokens = rows * n
    chunks = 7 if units % (7 * 128) == 0 else 1
    unit = units // chunks
    group = depth_n * row_n
    half = jnp.bfloat16
    hbm = pl.BlockSpec(memory_space=pl.ANY)
    vmem = pl.BlockSpec(memory_space=pltpu.VMEM)
    small = jax.ShapeDtypeStruct((rows, units), half)
    dma = pltpu.SemaphoreType.DMA
    return pl.pallas_call(
        functools.partial(exchange_kernel, (n, depth_n, row_n, chunks)),
        out_shape=[
            jax.ShapeDtypeStruct((tokens, units), half),
            jax.ShapeDtypeStruct((tokens, features), half),
            small, small, small,
        ],
        in_specs=[hbm, hbm, hbm],
        out_specs=[hbm, hbm, vmem, vmem, vmem],
        scratch_shapes=[
            pltpu.VMEM((tokens, features), half),
            pltpu.VMEM((chunks, unit, features), half),
            pltpu.VMEM((chunks, tokens, unit), half),
            pltpu.VMEM((2, chunks, n, rows, unit), half),
            dma, dma, dma((chunks,)), dma,
            dma((group // 2,)), dma((group // 2,)), dma((group // 2,)), dma((group // 2,)),
            dma((2, n - 1, HALVES)), dma((2, n - 1, HALVES)),
            dma((2, chunks, n)), dma((2, chunks, n)),
        ],
        compiler_params=pltpu.CompilerParams(
            collective_id=0, has_side_effects=True, vmem_limit_bytes=VMEM_BYTES),
        cost_estimate=pl.CostEstimate(
            flops=2 * tokens * units * features, bytes_accessed=2 * units * features, transcendentals=0),
    )(hidden, upstream, weight)


def local(sizes, hidden, upstream, weight):
    n, depth_n, row_n = sizes
    hidden_all, upstream_all, own, to_right, to_left = exchange(hidden, upstream, weight, n, depth_n, row_n)
    from_left = lax.ppermute(to_right, "col", [(i, i + 1) for i in range(n - 1)])
    from_right = lax.ppermute(to_left, "col", [(i + 1, i) for i in range(n - 1)])
    summed_weight = lax.dot_general(
        hidden_all, upstream_all, (((0,), (0,)), ((), ())), preferred_element_type=jnp.float32)
    token_scale = 1.0 / math.sqrt(hidden_all.shape[0])
    weight_grad = (summed_weight * token_scale).astype(jnp.bfloat16)
    wide = jnp.float32
    input_grad = (own.astype(wide) + from_left.astype(wide) + from_right.astype(wide)).astype(jnp.bfloat16)
    return (input_grad, weight_grad)


def solution(mesh):
    sizes = (mesh.shape["col"], mesh.shape["depth"], mesh.shape["row"])
    in_specs = (P("col", ("depth", "row")), P(("depth", "row"), "col"), P(("depth", "row"), "col"))
    out_specs = (P("col", ("depth", "row")), P(("depth", "row"), "col"))
    return jax.shard_map(
        functools.partial(local, sizes), mesh=mesh, in_specs=in_specs, out_specs=out_specs, check_vma=False)
```

time: 260 us -> 107 us (0.41)
  waiting for transfers between devices: 191 us -> 0.01 us
  Pallas kernels: 0 us -> 76.8 us
  matrix products: 41.7 us -> 21.3 us
  between operations: 13.7 us -> 0.67 us
  local copies, waits for them, and re-layouts: 9.16 us -> 0.01 us
    all_gather x2 -> x0, waiting for transfers between devices: 122 us -> none  [the longest x1 82.6 us: local(): lax.all_gather(hidden, 'col', axis=0, tiled=True)]
    pallas_call x0 -> x1, Pallas kernels: none -> 76.8 us  [exchange(): pl.pallas_call(functools.partial(exchange_kernel, (n, depth_n, row_n, chu...]
    unnamed x4 -> x0, waiting for transfers between devices: 69.2 us -> none
    dot_general x2 -> x1, matrix products: 41.7 us -> 21.3 us  [local(): lax.dot_general(hidden_all, upstream_all, (((0,), (0,)), ((), ())), prefe...]
    unnamed x2, local copies, waits for them, and re-layouts: 8.16 us -> 0.01 us
    ppermute x0 -> x2, starting transfers between devices: none -> 5.91 us  [the longest x1 4.61 us: local(): lax.ppermute(to_right, 'col', [(i, i + 1) for i in range(n - 1)])]
    all_to_all x1 -> x0, starting transfers between devices: 4.05 us -> none  [local(): lax.all_to_all(unit_share, 'col', split_axis=0, concat_axis=1, tiled=True)]
  transfers between devices with their start and end apart: 4 -> 2, of which waited for: 3 -> 0; matrix products, arithmetic and copies ran while one was open for 9% -> 20% of each run, Pallas kernels for 0% -> 0%
where the time goes in v1:
time: 107 us; the launch traced here: 106 us
  Pallas kernels  76.8 us (72%)
  matrix products  21.3 us (20%)
  starting transfers between devices  5.91 us (6%)
  other arithmetic  1.25 us (1%)
    pallas_call x1, Pallas kernels, exchange(): pl.pallas_call(functools.partial(exchange_kernel, (n, depth_n, row_n, chu...  76.8 us
    dot_general x1, matrix products, local(): lax.dot_general(hidden_all, upstream_all, (((0,), (0,)), ((), ())), prefe...  21.3 us
    ppermute x1, starting transfers between devices, local(): lax.ppermute(to_right, 'col', [(i, i + 1) for i in range(n - 1)])  4.61 us
  transfers between devices with their start and end apart: 2, of which 0 were waited for; matrix products, arithmetic and copies ran while one was open for 20% of the time, Pallas kernels for 0%

profile of v1, /device:TPU:0, one launch (start us, length us, event | category | flops | bytes accessed | tf_op | source)
XLA Modules:
  0.0 106.0 jit_solution(7197967876425487135)
XLA Ops:
  0.6 76.8 %shard_map.50 = (bf16[512,3584]{1,0:T(8,128)(2,1)}, bf16[512,3584]{1,0:T(8,128)(2,1)}, bf16[128,3584]{1,0:T(8,128)(2,1)}, bf16[128,3584]{1,0:T(8,128)(2,1)}, bf16[128,3584]{1,0:T(8,128)(2,1)}) custom-call(bf16[128,3584]{1,0:T(8,128)(2,1)} %hid.1, bf16[64,3584]{1,0:T(8,128)(2,1)} %up.1, bf16[3584,3584]{1,0:T(8,128)(2,1)} %w.1), custom_call_target="tpu_custom_call" | custom-call | flops 13153337344 | bytes 25690112 | tf_op jit(solution)/shard_map/pallas_call | solution.py:251
  77.4 4.6 %collective-permute-start = (bf16[128,3584]{1,0:T(8,128)(2,1)}, bf16[128,3584]{1,0:T(8,128)(2,1)S(1)}, u32[]{:S(2)}, u32[]{:S(2)}) collective-permute-start(bf16[128,3584]{1,0:T(8,128)(2,1)} %get-tuple-element.8), channel_id=1, source_target_pairs={{0,1},{1,2},{2,3},{4,5},{5,6},{6,7},{8,9},{9,10},{10,11},{12,13},{... | collective-permute-start | bytes 2752520 | tf_op jit(solution)/shard_map/ppermute | solution.py:280
  82.1 1.3 %collective-permute-start.1 = (bf16[128,3584]{1,0:T(8,128)(2,1)}, bf16[128,3584]{1,0:T(8,128)(2,1)S(1)}, u32[]{:S(2)}, u32[]{:S(2)}) collective-permute-start(bf16[128,3584]{1,0:T(8,128)(2,1)} %get-tuple-element.9), channel_id=1, source_target_pairs={{1,0},{2,1},{3,2},{5,4},{6,5},{7,6},{9,8},{10,9},{11,10},{13,12},{... | collective-permute-start | bytes 2752520 | tf_op jit(solution)/shard_map/ppermute | solution.py:281
  83.4 0.0 copy-start
  83.4 21.3 %multiply_convert_fusion = bf16[3584,3584]{1,0:T(8,128)(2,1)} fusion(bf16[512,3584]{1,0:T(8,128)(2,1)} %get-tuple-element.10, bf16[512,3584]{1,0:T(8,128)(2,1)} %get-tuple-element.11), kind=kOutput, calls=%fused_computation | convolution fusion | flops 13179027456 | bytes 33030144 | tf_op jit(solution)/shard_map/dot_general | solution.py:282
  104.7 0.0 collective-permute-done
  104.7 0.0 collective-permute-done.1
  104.7 0.0 copy-done
  104.7 1.3 %add_convert_fusion = bf16[128,3584]{1,0:T(8,128)(2,1)} fusion(bf16[128,3584]{1,0:T(8,128)(2,1)S(1)} %collective-permute-done.1, bf16[128,3584]{1,0:T(8,128)(2,1)S(1)} %collective-permute-done, bf16[128,3584]{1,0:T(8,128)(2,1)S(1)} %copy-done), kind=kLoop, calls=%fused_computation.1 | loop fusion | flops 2752512 | bytes 3670016 | tf_op jit(solution)/shard_map/convert_element_type | solution.py:287
Async XLA Ops:
  77.4 27.3 %collective-permute-start = (bf16[128,3584]{1,0:T(8,128)(2,1)}, bf16[128,3584]{1,0:T(8,128)(2,1)S(1)}, u32[]{:S(2)}, u32[]{:S(2)}) collective-permute-start(bf16[128,3584]{1,0:T(8,128)(2,1)} %get-tuple-element.8), channel_id=1, source_target_pairs={{0,1},{1,2},{2,3},{4,5},{5,6},{6,7},{8,9},{9,10},{10,11},{12,13},{... | collective-permute-start | bytes 2752520 | tf_op jit(solution)/shard_map/ppermute | solution.py:280
  82.1 22.7 %collective-permute-start.1 = (bf16[128,3584]{1,0:T(8,128)(2,1)}, bf16[128,3584]{1,0:T(8,128)(2,1)S(1)}, u32[]{:S(2)}, u32[]{:S(2)}) collective-permute-start(bf16[128,3584]{1,0:T(8,128)(2,1)} %get-tuple-element.9), channel_id=1, source_target_pairs={{1,0},{2,1},{3,2},{5,4},{6,5},{7,6},{9,8},{10,9},{11,10},{13,12},{... | collective-permute-start | bytes 2752520 | tf_op jit(solution)/shard_map/ppermute | solution.py:281
  83.4 21.4 %copy-start = (bf16[128,3584]{1,0:T(8,128)(2,1)S(1)}, bf16[128,3584]{1,0:T(8,128)(2,1)}, u32[]{:S(2)}) copy-start(bf16[128,3584]{1,0:T(8,128)(2,1)} %get-tuple-element.7) | copy-start | bytes 2752516

commit v2 on v1

--- a/solution.py
+++ b/solution.py
@@ -11,29 +11,31 @@
 MESH = pl.DeviceIdType.MESH
 HALVES = 2
 LAG = 2
+SLOTS = (0, 4)
 VMEM_BYTES = 60 * 1024 * 1024
 
 
 def exchange_kernel(
     sizes, hid, up, w, hall, uall, own, to_right, to_left,
-    up_all, w_all, part, got,
+    up_all, w_all, part, got, hid_own,
     up_local, hid_local, w_sem, out_sem,
-    up_send, up_recv, fwd_send, fwd_recv,
+    x_send, x_recv, y_send, y_recv, turn_send, turn_recv, core_send, core_recv,
     ag_send, ag_recv, rs_send, rs_recv,
 ):
     n, depth_n, row_n, chunks = sizes
-    group = depth_n * row_n
-    pairs = group // 2
+    pair_n = row_n // 2
     rows = hid.shape[0]
     up_rows = up.shape[0]
     unit = part.shape[2]
     half = rows // HALVES
     depth, row, z = lax.axis_index("depth"), lax.axis_index("row"), lax.axis_index("col")
-    me = depth * row_n + row
-    partner = me + 1 - 2 * lax.rem(me, 2)
-
-    def plane(i):
-        return (lax.div(i, row_n), lax.rem(i, row_n), z)
+    core, pair = lax.rem(row, 2), lax.div(row, 2)
+
+    def plane(a, b, c):
+        return (lax.rem(depth + a, depth_n), 2 * lax.rem(pair + b, pair_n) + c, z)
+
+    def source(a, b, c):
+        return lax.rem(depth - a + depth_n, depth_n) * row_n + 2 * lax.rem(pair - b + pair_n, pair_n) + c
 
     def line(way):
         return (depth, row, jnp.clip(z + (1 - 2 * way), 0, n - 1))
@@ -44,29 +46,40 @@
         return e if way == 0 else n - 1 - e
 
     barrier = pltpu.get_barrier_semaphore()
-    for k in range(1, pairs):
-        pl.semaphore_signal(barrier, inc=1, device_id=plane(lax.rem(me + 2 * k, group)), device_id_type=MESH)
-    pl.semaphore_signal(barrier, inc=1, device_id=plane(partner), device_id_type=MESH)
+    peers = [plane(a, 0, core) for a in range(1, depth_n)]
+    peers += [plane(0, b, core) for b in range(1, pair_n)]
+    peers += [plane(0, 0, 1 - core)]
+    for peer in peers:
+        pl.semaphore_signal(barrier, inc=1, device_id=peer, device_id_type=MESH)
     for way in range(2):
         @pl.when(place[way] < n - 1)
         def _():
             pl.semaphore_signal(barrier, inc=1, device_id=line(way), device_id_type=MESH)
     near = jnp.where(z > 0, 1, 0) + jnp.where(z < n - 1, 1, 0)
-    pl.semaphore_wait(barrier, pairs + near)
-
-    def up_at(i):
-        return up_all.at[pl.ds(pl.multiple_of(i * up_rows, up_rows), up_rows), :]
-
-    def up_copy(k, source):
+    pl.semaphore_wait(barrier, len(peers) + near)
+
+    def up_at(i, first=0, count=None):
+        count = up_rows if count is None else count
+        return up_all.at[pl.ds(pl.multiple_of(i * up_rows + first, count), count), :]
+
+    def remote(src, dst, send, recv, peer):
         return pltpu.make_async_remote_copy(
-            src_ref=up, dst_ref=up_at(source), send_sem=up_send.at[k], recv_sem=up_recv.at[k],
-            device_id=plane(lax.rem(me + 2 * k, group)), device_id_type=MESH)
-
-    def fwd_copy(k, source, first=False):
-        return pltpu.make_async_remote_copy(
-            src_ref=up if first else up_at(source), dst_ref=up_at(source),
-            send_sem=fwd_send.at[k], recv_sem=fwd_recv.at[k],
-            device_id=plane(partner), device_id_type=MESH)
+            src_ref=src, dst_ref=dst, send_sem=send, recv_sem=recv, device_id=peer, device_id_type=MESH)
+
+    def x_copy(a, i):
+        return remote(up, up_at(i), x_send.at[a], x_recv.at[a], plane(a, 0, core))
+
+    def y_copy(b, i):
+        return remote(up, up_at(i), y_send.at[b], y_recv.at[b], plane(0, b, core))
+
+    def turn_copy(part_of, a, b, i):
+        piece = up_at(i, part_of * (up_rows // 2), up_rows // 2)
+        peer = plane(0, b, core) if part_of == 0 else plane(a, 0, core)
+        return remote(piece, piece, turn_send.at[part_of, a, b], turn_recv.at[part_of, a, b], peer)
+
+    def core_copy(a, b, i):
+        src = up if a == 0 and b == 0 else up_at(i)
+        return remote(src, up_at(i), core_send.at[a, b], core_recv.at[a, b], plane(0, 0, 1 - core))
 
     def hid_rows(ref, b, c):
         return ref.at[pl.ds(pl.multiple_of(b * rows + c * half, half), half), :]
@@ -88,27 +101,25 @@
 
     def ag_pass(s, c):
         for way in range(2):
-            p = place[way]
-
-            @pl.when(p >= s)
+            @pl.when((place[way] >= s) & (place[way] < n - 1))
             def _():
                 ag_arrive(way, s, c)
-                if s + 1 <= n - 1:
-                    @pl.when(p < n - 1)
-                    def _():
-                        ag_copy(way, s + 1, c).start()
+                ag_copy(way, s + 1, c).start()
 
     for c in range(HALVES):
         for way in range(2):
             @pl.when(place[way] < n - 1)
             def _():
                 ag_copy(way, 1, c).start()
-    for k in range(1, pairs):
-        up_copy(k, me).start()
-    fwd_copy(0, me, True).start()
-    own_up = pltpu.make_async_copy(up, up_at(me), up_local)
+    mine = source(0, 0, core)
+    for a in range(1, depth_n):
+        x_copy(a, mine).start()
+    for b in range(1, pair_n):
+        y_copy(b, mine).start()
+    core_copy(0, 0, mine).start()
+    own_up = pltpu.make_async_copy(up, up_at(mine), up_local)
     own_up.start()
-    own_hid = pltpu.make_async_copy(hid, hall.at[pl.ds(pl.multiple_of(z * rows, rows), rows), :], hid_local)
+    own_hid = pltpu.make_async_copy(hid, hid_own, hid_local)
     own_hid.start()
 
     def w_copy(j):
@@ -118,16 +129,34 @@
     for j in range(chunks):
         w_copy(j).start()
 
-    for k in range(1, pairs):
-        source = lax.rem(me - 2 * k + group, group)
-        up_copy(k, source).wait_recv()
-        fwd_copy(k, source).start()
-    for c in range(HALVES):
-        if n > 1:
-            ag_pass(1, c)
+    own_hid.wait()
+    keep_hid = pltpu.make_async_copy(
+        hid_own, hall.at[pl.ds(pl.multiple_of(z * rows, rows), rows), :], hid_local)
+    keep_hid.start()
+    for a in range(1, depth_n):
+        i = source(a, 0, core)
+        x_copy(a, i).wait_recv()
+        for b in range(1, pair_n):
+            turn_copy(0, a, b, i).start()
+        core_copy(a, 0, i).start()
+    for b in range(1, pair_n):
+        i = source(0, b, core)
+        y_copy(b, i).wait_recv()
+        for a in range(1, depth_n):
+            turn_copy(1, a, b, i).start()
+        core_copy(0, b, i).start()
+    for c in range(HALVES - 1):
+        ag_pass(1, c)
+    for a in range(1, depth_n):
+        for b in range(1, pair_n):
+            i = source(a, b, core)
+            turn_copy(0, a, b, i).wait_recv()
+            turn_copy(1, a, b, i).wait_recv()
+            core_copy(a, b, i).start()
     own_up.wait()
-    for k in range(pairs):
-        fwd_copy(k, lax.rem(partner - 2 * k + group, group)).wait_recv()
+    for a in range(depth_n):
+        for b in range(pair_n):
+            core_copy(a, b, source(a, b, 1 - core)).wait_recv()
     keep_up = pltpu.make_async_copy(up_all, uall, out_sem)
     keep_up.start()
 
@@ -152,8 +181,8 @@
             part_at(j, b)[...] = rs_add(way, j, b)
         rs_copy(way, j, b).start()
 
-    later = [(s, c) for s in range(2, n) for c in range(HALVES)]
-    slot_of = [min(1 + 3 * i, chunks - 1) for i in range(len(later))]
+    later = [(1, HALVES - 1)] + [(s, c) for s in range(2, n - 1) for c in range(HALVES)]
+    slot_of = [min(SLOTS[i], chunks - 1) if i < len(SLOTS) else chunks - 1 for i in range(len(later))]
 
     @pl.loop(0, chunks)
     def _(j):
@@ -179,7 +208,7 @@
                     ag_pass(s, c)
 
     for (s, c), slot in zip(later, slot_of):
-        if slot >= chunks - 1 and s < n - 1:
+        if slot >= chunks - 1:
             ag_pass(s, c)
 
     @pl.loop(max(chunks - LAG, 0), chunks)
@@ -212,14 +241,23 @@
             def _():
                 out[:, columns] = part_at(j, b)[...]
 
-    for (s, c), slot in zip(later, slot_of):
-        if slot >= chunks - 1 and s == n - 1:
-            ag_pass(s, c)
-
-    for k in range(1, pairs):
-        up_copy(k, me).wait_send()
-    for k in range(pairs):
-        fwd_copy(k, lax.rem(me - 2 * k + group, group), k == 0).wait_send()
+    for way in range(2):
+        for s in range(1, n):
+            @pl.when((place[way] >= s) & ((place[way] == n - 1) | (s == n - 1)))
+            def _():
+                for c in range(HALVES):
+                    ag_arrive(way, s, c)
+
+    for a in range(depth_n):
+        for b in range(pair_n):
+            core_copy(a, b, source(a, b, core)).wait_send()
+            if a and not b:
+                x_copy(a, mine).wait_send()
+            if b and not a:
+                y_copy(b, mine).wait_send()
+            if a and b:
+                turn_copy(0, a, b, source(a, 0, core)).wait_send()
+                turn_copy(1, a, b, source(0, b, core)).wait_send()
     for way in range(2):
         for s in range(1, n):
             @pl.when((place[way] >= s - 1) & (place[way] < n - 1))
@@ -232,7 +270,7 @@
                 @pl.loop(0, chunks)
                 def _(j):
                     rs_copy(way, j, block_of(way, e)).wait_send()
-    own_hid.wait()
+    keep_hid.wait()
     keep_up.wait()
 
 
@@ -242,7 +280,7 @@
     tokens = rows * n
     chunks = 7 if units % (7 * 128) == 0 else 1
     unit = units // chunks
-    group = depth_n * row_n
+    pair_n = row_n // 2
     half = jnp.bfloat16
     hbm = pl.BlockSpec(memory_space=pl.ANY)
     vmem = pl.BlockSpec(memory_space=pltpu.VMEM)
@@ -262,8 +300,10 @@
             pltpu.VMEM((chunks, unit, features), half),
             pltpu.VMEM((chunks, tokens, unit), half),
             pltpu.VMEM((2, chunks, n, rows, unit), half),
+            pltpu.VMEM((rows, units), half),
             dma, dma, dma((chunks,)), dma,
-            dma((group // 2,)), dma((group // 2,)), dma((group // 2,)), dma((group // 2,)),
+            dma((depth_n,)), dma((depth_n,)), dma((pair_n,)), dma((pair_n,)),
+            dma((2, depth_n, pair_n)), dma((2, depth_n, pair_n)), dma((depth_n, pair_n)), dma((depth_n, pair_n)),
             dma((2, n - 1, HALVES)), dma((2, n - 1, HALVES)),
             dma((2, chunks, n)), dma((2, chunks, n)),
         ],
@@ -274,15 +314,41 @@
     )(hidden, upstream, weight)
 
 
+def weight_kernel(scale, hid, up, out):
+    width = out.shape[1]
+    step = 512 if width % 512 == 0 else 128
+    for first in range(0, width, step):
+        columns = slice(first, first + step)
+        summed = lax.dot_general(
+            hid[...], up[:, columns], (((0,), (0,)), ((), ())), preferred_element_type=jnp.float32)
+        out[:, columns] = (summed * scale).astype(out.dtype)
+
+
+def weight_gradient(hidden_all, upstream_all):
+    tokens, units = hidden_all.shape
+    features = upstream_all.shape[1]
+    unit = 512 if units % 512 == 0 else 128
+    return pl.pallas_call(
+        functools.partial(weight_kernel, 1.0 / math.sqrt(tokens)),
+        grid=(units // unit,),
+        in_specs=[
+            pl.BlockSpec((tokens, unit), lambda i: (0, i)),
+            pl.BlockSpec((tokens, features), lambda i: (0, 0)),
+        ],
+        out_specs=pl.BlockSpec((unit, features), lambda i: (i, 0)),
+        out_shape=jax.ShapeDtypeStruct((units, features), jnp.bfloat16),
+        compiler_params=pltpu.CompilerParams(vmem_limit_bytes=VMEM_BYTES),
+        cost_estimate=pl.CostEstimate(
+            flops=2 * tokens * units * features, bytes_accessed=2 * units * features, transcendentals=0),
+    )(hidden_all, upstream_all)
+
+
 def local(sizes, hidden, upstream, weight):
     n, depth_n, row_n = sizes
     hidden_all, upstream_all, own, to_right, to_left = exchange(hidden, upstream, weight, n, depth_n, row_n)
     from_left = lax.ppermute(to_right, "col", [(i, i + 1) for i in range(n - 1)])
     from_right = lax.ppermute(to_left, "col", [(i + 1, i) for i in range(n - 1)])
-    summed_weight = lax.dot_general(
-        hidden_all, upstream_all, (((0,), (0,)), ((), ())), preferred_element_type=jnp.float32)
-    token_scale = 1.0 / math.sqrt(hidden_all.shape[0])
-    weight_grad = (summed_weight * token_scale).astype(jnp.bfloat16)
+    weight_grad = weight_gradient(hidden_all, upstream_all)
     wide = jnp.float32
     input_grad = (own.astype(wide) + from_left.astype(wide) + from_right.astype(wide)).astype(jnp.bfloat16)
     return (input_grad, weight_grad)

time: 107 us -> 98.8 us (0.923)
  matrix products: 21.3 us -> 0 us
  Pallas kernels: 76.8 us -> 86.6 us
  waiting for transfers between devices: 0.01 us -> 5.34 us
  starting transfers between devices: 5.91 us -> 4.76 us
    dot_general x1 -> x0, matrix products: 21.3 us -> none  [local(): lax.dot_general(hidden_all, upstream_all, (((0,), (0,)), ((), ())), prefe...]
    pallas_call x0 -> x1, Pallas kernels: none -> 18.9 us  [weight_gradient(): pl.pallas_call(functools.partial(weight_kernel, 1.0 / math.sqrt(tokens)),...]
    pallas_call x1, Pallas kernels: 76.8 us -> 67.7 us  [exchange(): pl.pallas_call(functools.partial(exchange_kernel, (n, depth_n, row_n, chu...]
    ppermute x1, waiting for transfers between devices: 0.01 us -> 5.18 us  [local(): lax.ppermute(to_left, 'col', [(i + 1, i) for i in range(n - 1)])]
    ppermute x1, starting transfers between devices: 4.61 us -> 3.47 us  [local(): lax.ppermute(to_right, 'col', [(i, i + 1) for i in range(n - 1)])]
  transfers between devices with their start and end apart: 2 -> 2, of which waited for: 0 -> 2; matrix products, arithmetic and copies ran while one was open for 20% -> 0% of each run, Pallas kernels for 0% -> 19%
where the time goes in v2:
time: 98.8 us; the launch traced here: 98.6 us
  Pallas kernels  86.6 us (88%)
  waiting for transfers between devices  5.34 us (5%)
  starting transfers between devices  4.76 us (5%)
  other arithmetic  1.25 us (1%)
    pallas_call x1, Pallas kernels, exchange(): pl.pallas_call(functools.partial(exchange_kernel, (n, depth_n, row_n, chu...  67.7 us
    pallas_call x1, Pallas kernels, weight_gradient(): pl.pallas_call(functools.partial(weight_kernel, 1.0 / math.sqrt(tokens)),...  18.9 us
    ppermute x1, waiting for transfers between devices, local(): lax.ppermute(to_left, 'col', [(i + 1, i) for i in range(n - 1)])  5.18 us
    ppermute x1, starting transfers between devices, local(): lax.ppermute(to_right, 'col', [(i, i + 1) for i in range(n - 1)])  3.47 us
  transfers between devices with their start and end apart: 2, of which 2 were waited for; matrix products, arithmetic and copies ran while one was open for 0% of the time, Pallas kernels for 19%

profile of v2, /device:TPU:0, one launch (start us, length us, event | category | flops | bytes accessed | tf_op | source)
XLA Modules:
  0.0 98.6 jit_solution(6361711198235173820)
XLA Ops:
  0.6 67.7 %shard_map.50 = (bf16[512,3584]{1,0:T(8,128)(2,1)}, bf16[512,3584]{1,0:T(8,128)(2,1)}, bf16[128,3584]{1,0:T(8,128)(2,1)}, bf16[128,3584]{1,0:T(8,128)(2,1)}, bf16[128,3584]{1,0:T(8,128)(2,1)}) custom-call(bf16[128,3584]{1,0:T(8,128)(2,1)} %hid.1, bf16[64,3584]{1,0:T(8,128)(2,1)} %up.1, bf16[3584,3584]{1,0:T(8,128)(2,1)} %w.1), custom_call_target="tpu_custom_call" | custom-call | flops 13153337344 | bytes 25690112 | tf_op jit(solution)/shard_map/pallas_call | solution.py:289
  68.3 3.5 %collective-permute-start = (bf16[128,3584]{1,0:T(8,128)(2,1)}, bf16[128,3584]{1,0:T(8,128)(2,1)S(1)}, u32[]{:S(2)}, u32[]{:S(2)}) collective-permute-start(bf16[128,3584]{1,0:T(8,128)(2,1)} %get-tuple-element.8), channel_id=1, source_target_pairs={{0,1},{1,2},{2,3},{4,5},{5,6},{6,7},{8,9},{9,10},{10,11},{12,13},{... | collective-permute-start | bytes 2752520 | tf_op jit(solution)/shard_map/ppermute | solution.py:349
  71.8 1.3 %collective-permute-start.1 = (bf16[128,3584]{1,0:T(8,128)(2,1)}, bf16[128,3584]{1,0:T(8,128)(2,1)S(1)}, u32[]{:S(2)}, u32[]{:S(2)}) collective-permute-start(bf16[128,3584]{1,0:T(8,128)(2,1)} %get-tuple-element.9), channel_id=1, source_target_pairs={{1,0},{2,1},{3,2},{5,4},{6,5},{7,6},{9,8},{10,9},{11,10},{13,12},{... | collective-permute-start | bytes 2752520 | tf_op jit(solution)/shard_map/ppermute | solution.py:350
  73.1 0.0 copy-start
  73.1 18.9 %shard_map.51 = bf16[3584,3584]{1,0:T(8,128)(2,1)} custom-call(bf16[512,3584]{1,0:T(8,128)(2,1)} %get-tuple-element.10.hid, bf16[512,3584]{1,0:T(8,128)(2,1)} %get-tuple-element.11.up), custom_call_target="tpu_custom_call" | custom-call | flops 13153337344 | bytes 25690112 | tf_op jit(solution)/shard_map/pallas_call | solution.py:331
  92.0 0.2 collective-permute-done
  92.2 5.2 %collective-permute-done.1 = bf16[128,3584]{1,0:T(8,128)(2,1)S(1)} collective-permute-done((bf16[128,3584]{1,0:T(8,128)(2,1)}, bf16[128,3584]{1,0:T(8,128)(2,1)S(1)}, u32[]{:S(2)}, u32[]{:S(2)}) %collective-permute-start.1) | collective-permute-done | bytes 917536 | tf_op jit(solution)/shard_map/ppermute | solution.py:350
  97.4 0.0 copy-done
  97.4 1.3 %add_convert_fusion = bf16[128,3584]{1,0:T(8,128)(2,1)} fusion(bf16[128,3584]{1,0:T(8,128)(2,1)S(1)} %collective-permute-done.1, bf16[128,3584]{1,0:T(8,128)(2,1)S(1)} %collective-permute-done, bf16[128,3584]{1,0:T(8,128)(2,1)S(1)} %copy-done), kind=kLoop, calls=%fused_computation | loop fusion | flops 2752512 | bytes 3670016 | tf_op jit(solution)/shard_map/convert_element_type | solution.py:353
Async XLA Ops:
  68.3 23.9 %collective-permute-start = (bf16[128,3584]{1,0:T(8,128)(2,1)}, bf16[128,3584]{1,0:T(8,128)(2,1)S(1)}, u32[]{:S(2)}, u32[]{:S(2)}) collective-permute-start(bf16[128,3584]{1,0:T(8,128)(2,1)} %get-tuple-element.8), channel_id=1, source_target_pairs={{0,1},{1,2},{2,3},{4,5},{5,6},{6,7},{8,9},{9,10},{10,11},{12,13},{... | collective-permute-start | bytes 2752520 | tf_op jit(solution)/shard_map/ppermute | solution.py:349
  71.8 25.6 %collective-permute-start.1 = (bf16[128,3584]{1,0:T(8,128)(2,1)}, bf16[128,3584]{1,0:T(8,128)(2,1)S(1)}, u32[]{:S(2)}, u32[]{:S(2)}) collective-permute-start(bf16[128,3584]{1,0:T(8,128)(2,1)} %get-tuple-element.9), channel_id=1, source_target_pairs={{1,0},{2,1},{3,2},{5,4},{6,5},{7,6},{9,8},{10,9},{11,10},{13,12},{... | collective-permute-start | bytes 2752520 | tf_op jit(solution)/shard_map/ppermute | solution.py:350
  73.1 24.3 %copy-start = (bf16[128,3584]{1,0:T(8,128)(2,1)S(1)}, bf16[128,3584]{1,0:T(8,128)(2,1)}, u32[]{:S(2)}) copy-start(bf16[128,3584]{1,0:T(8,128)(2,1)} %get-tuple-element.7) | copy-start | bytes 2752516

commit v3 on v2

--- a/solution.py
+++ b/solution.py
@@ -106,17 +106,17 @@
                 ag_arrive(way, s, c)
                 ag_copy(way, s + 1, c).start()
 
-    for c in range(HALVES):
-        for way in range(2):
-            @pl.when(place[way] < n - 1)
-            def _():
-                ag_copy(way, 1, c).start()
     mine = source(0, 0, core)
     for a in range(1, depth_n):
         x_copy(a, mine).start()
     for b in range(1, pair_n):
         y_copy(b, mine).start()
     core_copy(0, 0, mine).start()
+    for c in range(HALVES):
+        for way in range(2):
+            @pl.when(place[way] < n - 1)
+            def _():
+                ag_copy(way, 1, c).start()
     own_up = pltpu.make_async_copy(up, up_at(mine), up_local)
     own_up.start()
     own_hid = pltpu.make_async_copy(hid, hid_own, hid_local)

time: 98.8 us -> 98.8 us (level)
  no operation moved by 1% of the time
where the time goes in v3:
time: 98.8 us; the launch traced here: 98.6 us
  Pallas kernels  86.6 us (88%)
  waiting for transfers between devices  5.3 us (5%)
  starting transfers between devices  4.75 us (5%)
  other arithmetic  1.25 us (1%)
    pallas_call x1, Pallas kernels, exchange(): pl.pallas_call(functools.partial(exchange_kernel, (n, depth_n, row_n, chu...  67.7 us
    pallas_call x1, Pallas kernels, weight_gradient(): pl.pallas_call(functools.partial(weight_kernel, 1.0 / math.sqrt(tokens)),...  18.9 us
    ppermute x1, waiting for transfers between devices, local(): lax.ppermute(to_left, 'col', [(i + 1, i) for i in range(n - 1)])  5.17 us
    ppermute x1, starting transfers between devices, local(): lax.ppermute(to_right, 'col', [(i, i + 1) for i in range(n - 1)])  3.46 us
  transfers between devices with their start and end apart: 2, of which 2 were waited for; matrix products, arithmetic and copies ran while one was open for 0% of the time, Pallas kernels for 19%

profile of v3, /device:TPU:0, one launch (start us, length us, event | category | flops | bytes accessed | tf_op | source)
XLA Modules:
  0.0 98.6 jit_solution(5721939693805921416)
XLA Ops:
  0.6 67.7 %shard_map.50 = (bf16[512,3584]{1,0:T(8,128)(2,1)}, bf16[512,3584]{1,0:T(8,128)(2,1)}, bf16[128,3584]{1,0:T(8,128)(2,1)}, bf16[128,3584]{1,0:T(8,128)(2,1)}, bf16[128,3584]{1,0:T(8,128)(2,1)}) custom-call(bf16[128,3584]{1,0:T(8,128)(2,1)} %hid.1, bf16[64,3584]{1,0:T(8,128)(2,1)} %up.1, bf16[3584,3584]{1,0:T(8,128)(2,1)} %w.1), custom_call_target="tpu_custom_call" | custom-call | flops 13153337344 | bytes 25690112 | tf_op jit(solution)/shard_map/pallas_call | solution.py:289
  68.3 3.5 %collective-permute-start = (bf16[128,3584]{1,0:T(8,128)(2,1)}, bf16[128,3584]{1,0:T(8,128)(2,1)S(1)}, u32[]{:S(2)}, u32[]{:S(2)}) collective-permute-start(bf16[128,3584]{1,0:T(8,128)(2,1)} %get-tuple-element.8), channel_id=1, source_target_pairs={{0,1},{1,2},{2,3},{4,5},{5,6},{6,7},{8,9},{9,10},{10,11},{12,13},{... | collective-permute-start | bytes 2752520 | tf_op jit(solution)/shard_map/ppermute | solution.py:349
  71.8 1.3 %collective-permute-start.1 = (bf16[128,3584]{1,0:T(8,128)(2,1)}, bf16[128,3584]{1,0:T(8,128)(2,1)S(1)}, u32[]{:S(2)}, u32[]{:S(2)}) collective-permute-start(bf16[128,3584]{1,0:T(8,128)(2,1)} %get-tuple-element.9), channel_id=1, source_target_pairs={{1,0},{2,1},{3,2},{5,4},{6,5},{7,6},{9,8},{10,9},{11,10},{13,12},{... | collective-permute-start | bytes 2752520 | tf_op jit(solution)/shard_map/ppermute | solution.py:350
  73.1 0.0 copy-start
  73.1 18.9 %shard_map.51 = bf16[3584,3584]{1,0:T(8,128)(2,1)} custom-call(bf16[512,3584]{1,0:T(8,128)(2,1)} %get-tuple-element.10.hid, bf16[512,3584]{1,0:T(8,128)(2,1)} %get-tuple-element.11.up), custom_call_target="tpu_custom_call" | custom-call | flops 13153337344 | bytes 25690112 | tf_op jit(solution)/shard_map/pallas_call | solution.py:331
  92.0 0.1 collective-permute-done
  92.2 5.2 %collective-permute-done.1 = bf16[128,3584]{1,0:T(8,128)(2,1)S(1)} collective-permute-done((bf16[128,3584]{1,0:T(8,128)(2,1)}, bf16[128,3584]{1,0:T(8,128)(2,1)S(1)}, u32[]{:S(2)}, u32[]{:S(2)}) %collective-permute-start.1) | collective-permute-done | bytes 917536 | tf_op jit(solution)/shard_map/ppermute | solution.py:350
  97.3 0.0 copy-done
  97.3 1.3 %add_convert_fusion = bf16[128,3584]{1,0:T(8,128)(2,1)} fusion(bf16[128,3584]{1,0:T(8,128)(2,1)S(1)} %collective-permute-done.1, bf16[128,3584]{1,0:T(8,128)(2,1)S(1)} %collective-permute-done, bf16[128,3584]{1,0:T(8,128)(2,1)S(1)} %copy-done), kind=kLoop, calls=%fused_computation | loop fusion | flops 2752512 | bytes 3670016 | tf_op jit(solution)/shard_map/convert_element_type | solution.py:353
Async XLA Ops:
  68.3 23.8 %collective-permute-start = (bf16[128,3584]{1,0:T(8,128)(2,1)}, bf16[128,3584]{1,0:T(8,128)(2,1)S(1)}, u32[]{:S(2)}, u32[]{:S(2)}) collective-permute-start(bf16[128,3584]{1,0:T(8,128)(2,1)} %get-tuple-element.8), channel_id=1, source_target_pairs={{0,1},{1,2},{2,3},{4,5},{5,6},{6,7},{8,9},{9,10},{10,11},{12,13},{... | collective-permute-start | bytes 2752520 | tf_op jit(solution)/shard_map/ppermute | solution.py:349
  71.8 25.5 %collective-permute-start.1 = (bf16[128,3584]{1,0:T(8,128)(2,1)}, bf16[128,3584]{1,0:T(8,128)(2,1)S(1)}, u32[]{:S(2)}, u32[]{:S(2)}) collective-permute-start(bf16[128,3584]{1,0:T(8,128)(2,1)} %get-tuple-element.9), channel_id=1, source_target_pairs={{1,0},{2,1},{3,2},{5,4},{6,5},{7,6},{9,8},{10,9},{11,10},{13,12},{... | collective-permute-start | bytes 2752520 | tf_op jit(solution)/shard_map/ppermute | solution.py:350
  73.1 24.2 %copy-start = (bf16[128,3584]{1,0:T(8,128)(2,1)S(1)}, bf16[128,3584]{1,0:T(8,128)(2,1)}, u32[]{:S(2)}) copy-start(bf16[128,3584]{1,0:T(8,128)(2,1)} %get-tuple-element.7) | copy-start | bytes 2752516
